TPU v7x, 256 devices: a whole 4x4x8 slice. The times are simulated.
256 devices in a mesh: dp: 16 (over z, core), expert: 16 (over y, x).
Axes of the slice: x: 4, y: 4, z: 8, core: 2. Of those that a mesh axis runs over, the one named last changes fastest.
Arguments:
- tokens: bfloat16 [32768, 1024], P(('dp', 'expert')), may hold values from -6 to 6
- grad_out: bfloat16 [32768, 1024], P(('dp', 'expert')), may hold values from -6 to 6
- routes: int32 [32768, 10], P(('dp', 'expert')), may hold values from 0 to 47, all different within a row; in each aligned block of 128 rows (0 to 127, 128 to 255, ...) at most 32 rows name the same one
- combine: bfloat16 [32768, 10], P(('dp', 'expert')), may hold values from 0.049804688 to 0.29882812
- w_gate: bfloat16 [48, 1024, 512], P('expert'), may hold values from -0.1875 to 0.1875
- w_up: bfloat16 [48, 1024, 512], P('expert'), may hold values from -0.1875 to 0.1875
- w_down: bfloat16 [48, 512, 1024], P('expert'), may hold values from -0.25 to 0.25
Outputs:
- grad_tokens: bfloat16 [32768, 1024], P(('dp', 'expert'))
- grad_gate: bfloat16 [48, 1024, 512], P('expert', 'dp')
- grad_up: bfloat16 [48, 1024, 512], P('expert', 'dp')
- grad_down: bfloat16 [48, 512, 1024], P('expert', 'dp')
Inputs may be any that keep to these rules, and one draw needn't show every extreme that they name: `routes`: A token's 10 experts are different. Among the 128 tokens of one device no expert is named more than 32 times, a bound that some block reaches.
All inputs are finite; a program needn't handle non-finite values.
Results may differ from a plain program's by a relative error of at most 0.022.
Values may be sent and summed in bfloat16 or wider, within the bound.
A program may use at most 128 MiB of HBM per device.

v0:
```python
import jax
import jax.numpy as jnp
from jax import lax
from jax.sharding import PartitionSpec as P


def slot_ranks(route_block, expert_total):
    flat_ids = route_block.reshape(-1)
    marks = (flat_ids[:, None] == jnp.arange(expert_total, dtype=jnp.int32)[None, :]).astype(
        jnp.int32
    )
    return jnp.sum((jnp.cumsum(marks, axis=0) - 1) * marks, axis=1)


def build_slots(route_block, expert_total, slot_depth):
    flat_ids = route_block.reshape(-1)
    pair_total = flat_ids.shape[0]
    slot_rank = slot_ranks(route_block, expert_total)
    slots = jnp.full((expert_total, slot_depth), pair_total, dtype=jnp.int32)
    slots = slots.at[flat_ids, slot_rank].set(jnp.arange(pair_total, dtype=jnp.int32))
    return (slots, slot_rank)


def contract_last(left, right):
    return lax.dot_general(
        left, right, (((1,), (1,)), ((), ())), preferred_element_type=jnp.float32
    )


def contract_first(left, right):
    return lax.dot_general(
        left, right, (((0,), (0,)), ((), ())), preferred_element_type=jnp.float32
    )


def expert_backward(rows_x, rows_dy, rows_c, gate_w, up_w, down_w):
    gate_pre = jnp.dot(rows_x, gate_w, preferred_element_type=jnp.float32)
    up_pre = jnp.dot(rows_x, up_w, preferred_element_type=jnp.float32)
    sigmoid_gate = jax.nn.sigmoid(gate_pre)
    hidden = (gate_pre * sigmoid_gate * up_pre).astype(jnp.bfloat16)
    d_out = (rows_c[:, None] * rows_dy.astype(jnp.float32)).astype(jnp.bfloat16)
    d_hidden = contract_last(d_out, down_w)
    d_gate = (d_hidden * up_pre * sigmoid_gate * (1.0 + gate_pre * (1.0 - sigmoid_gate))).astype(
        jnp.bfloat16
    )
    d_up = (d_hidden * gate_pre * sigmoid_gate).astype(jnp.bfloat16)
    d_rows = (contract_last(d_gate, gate_w) + contract_last(d_up, up_w)).astype(jnp.bfloat16)
    return (hidden, d_out, d_gate, d_up, d_rows)


def shards(tokens, grad_out, routes, combine, w_gate, w_up, w_down):
    tok_dev, model_width = tokens.shape
    top_count = routes.shape[1]
    peer_count = lax.axis_size("expert")
    held_experts = w_gate.shape[0]
    hidden_units = w_gate.shape[2]
    expert_total = peer_count * held_experts
    slot_depth = 8 * ((tok_dev * top_count * 6 // (5 * expert_total) + 7) // 8)
    pair_total = tok_dev * top_count
    slots, slot_rank = build_slots(routes, expert_total, slot_depth)
    filled = slots < pair_total
    token_index = jnp.where(filled, slots // top_count, tok_dev)
    pad_row = jnp.zeros((1, model_width), jnp.bfloat16)
    send_x = jnp.concatenate([tokens, pad_row])[token_index].reshape(
        peer_count, held_experts, slot_depth, model_width
    )
    send_dy = jnp.concatenate([grad_out, pad_row])[token_index].reshape(
        peer_count, held_experts, slot_depth, model_width
    )
    weight_ext = jnp.concatenate([combine.reshape(-1), jnp.zeros((1,), jnp.bfloat16)])
    send_c = weight_ext[slots].reshape(peer_count, held_experts, slot_depth)
    recv_x, recv_dy, recv_c = (
        lax.all_to_all(send_x, "expert", split_axis=0, concat_axis=0, tiled=True),
        lax.all_to_all(send_dy, "expert", split_axis=0, concat_axis=0, tiled=True),
        lax.all_to_all(send_c, "expert", split_axis=0, concat_axis=0, tiled=True),
    )
    gate_parts = []
    up_parts = []
    down_parts = []
    row_list = []
    for which in range(held_experts):
        rows_x = recv_x[:, which].reshape(-1, model_width)
        rows_dy = recv_dy[:, which].reshape(-1, model_width)
        rows_c = recv_c[:, which].reshape(-1).astype(jnp.float32)
        hidden, d_out, d_gate, d_up, d_rows = expert_backward(
            rows_x, rows_dy, rows_c, w_gate[which], w_up[which], w_down[which]
        )
        d_both = jnp.concatenate([d_gate, d_up], axis=1)
        row_list.append(d_rows.reshape(peer_count, slot_depth, model_width))
        summed = lax.psum_scatter(
            contract_first(rows_x, d_both).astype(jnp.bfloat16),
            "dp",
            scatter_dimension=0,
            tiled=True,
        ).astype(jnp.float32)
        gate_parts.append(summed[:, :hidden_units].astype(jnp.bfloat16))
        up_parts.append(summed[:, hidden_units:].astype(jnp.bfloat16))
        down_parts.append(
            lax.psum_scatter(
                contract_first(hidden, d_out).astype(jnp.bfloat16),
                "dp",
                scatter_dimension=0,
                tiled=True,
            )
        )
    grad_gate = jnp.stack(gate_parts)
    grad_up = jnp.stack(up_parts)
    grad_down = jnp.stack(down_parts)
    stacked = jnp.stack(row_list, axis=1)
    returned = lax.all_to_all(stacked, "expert", split_axis=0, concat_axis=0, tiled=True)
    flat_back = returned.reshape(expert_total * slot_depth, model_width)
    row_of_pair = routes.reshape(-1) * slot_depth + slot_rank
    per_pair = flat_back[row_of_pair].astype(jnp.float32).reshape(tok_dev, top_count, model_width)
    grad_tokens = jnp.sum(per_pair, axis=1).astype(jnp.bfloat16)
    return (grad_tokens, grad_gate, grad_up, grad_down)


def solution(mesh):
    return jax.shard_map(
        shards,
        mesh=mesh,
        in_specs=(
            P(("dp", "expert"), None),
            P(("dp", "expert"), None),
            P(("dp", "expert"), None),
            P(("dp", "expert"), None),
            P("expert", None, None),
            P("expert", None, None),
            P("expert", None, None),
        ),
        out_specs=(
            P(("dp", "expert"), None),
            P("expert", "dp", None),
            P("expert", "dp", None),
            P("expert", "dp", None),
        ),
        check_vma=False,
    )
```

profile of v0, /device:TPU:2, one launch (start us, length us, event | category | flops | bytes accessed | tf_op | source)
XLA Modules:
  0.0 523.7 jit_solution(4750280314631814828)
XLA Ops:
  8.5 13.6 %reduce-window.6 = s32[48,10,128]{2,1,0:T(8,128)S(1)} reduce-window(s32[48,10,128]{2,1,0:T(8,128)S(1)} %fusion.57, s32[]{:T(128)} %constant.16.clone.1), window={size=1x1x128 pad=0_0x0_0x127_0}, to_apply=%region_0.0 | reduce-window | flops 7802880 | bytes 491524 | tf_op jit(solution)/shard_map/reduce-window
  23.1 5.2 %scatter_custom_fusion = s32[1536]{0:T(1024)S(1)} fusion(s32[1280]{0:T(1024)S(1)} %broadcast_select_fusion, s32[1280]{0:T(1024)S(1)} %iota.11, s32[]{:T(128)} %constant.15.clone.1), kind=kCustom, calls=%fused_computation.134 | custom fusion | bytes 6148
  29.0 9.5 %gather_fusion = bf16[1536]{0:T(1024)(128)(2,1)S(1)} fusion(bf16[1281]{0:T(1024)(128)(2,1)S(1)} %pad_maximum_fusion.4, s32[2048]{0:T(1024)S(1)} %pad_clamp_fusion.2), kind=kCustom, calls=%fused_computation | custom fusion | bytes 12288 | tf_op jit(solution)/shard_map/gather | solution.py:71
  39.2 7.5 %all-to-all-start = ((bf16[16,3,32]{2,1,0:T(4,128)(2,1)}), bf16[16,3,32]{2,1,0:T(4,128)(2,1)S(1)}, u32[]{:S(2)}, u32[]{:S(2)}) async-start(bf16[16,3,32]{2,1,0:T(4,128)(2,1)} %reshape.178), calls=%async_computation | async-start | bytes 32768 | tf_op jit(solution)/shard_map/all_to_all | solution.py:75
  46.8 5.8 %gather_fusion.2 = bf16[1536,1024]{1,0:T(8,128)(2,1)} fusion(bf16[129,1024]{1,0:T(8,128)(2,1)S(1)} %concatenate.24, s32[2048]{0:T(1024)S(1)} %pad_clamp_fusion.1), kind=kCustom, calls=%fused_computation.2 | custom fusion | bytes 6297600 | tf_op jit(solution)/shard_map/gather | solution.py:64
  52.9 7.1 %all-to-all-start.2 = ((bf16[16,3,32,1024]{3,2,1,0:T(8,128)(2,1)}), bf16[16,3,32,1024]{3,2,1,0:T(8,128)(2,1)S(1)}, u32[]{:S(2)}, u32[]{:S(2)}) async-start(bf16[16,3,32,1024]{3,2,1,0:T(8,128)(2,1)} %bitcast.7), calls=%async_computation.2 | async-start | bytes 6291456 | tf_op jit(solution)/shard_map/all_to_all | solution.py:73
  59.9 1.0 concatenate.23
  60.9 5.8 %gather_fusion.1 = bf16[1536,1024]{1,0:T(8,128)(2,1)} fusion(bf16[129,1024]{1,0:T(8,128)(2,1)S(1)} %concatenate.23, s32[2048]{0:T(1024)S(1)} %pad_clamp_fusion.1), kind=kCustom, calls=%fused_computation.1 | custom fusion | bytes 6297600 | tf_op jit(solution)/shard_map/gather | solution.py:67
  66.7 33.8 %all-to-all-done.2 = bf16[16,3,32,1024]{3,2,1,0:T(8,128)(2,1)S(1)} async-done(((bf16[16,3,32,1024]{3,2,1,0:T(8,128)(2,1)}), bf16[16,3,32,1024]{3,2,1,0:T(8,128)(2,1)S(1)}, u32[]{:S(2)}, u32[]{:S(2)}) %all-to-all-start.2) | async-done | bytes 3145760 | tf_op jit(solution)/shard_map/all_to_all | solution.py:73
  100.6 1.7 copy-done
  102.2 8.9 %all-to-all-start.1 = ((bf16[16,3,32,1024]{3,2,1,0:T(8,128)(2,1)}), bf16[16,3,32,1024]{3,2,1,0:T(8,128)(2,1)S(1)}, u32[]{:S(2)}, u32[]{:S(2)}) async-start(bf16[16,3,32,1024]{3,2,1,0:T(8,128)(2,1)} %bitcast.150), calls=%async_computation.1 | async-start | bytes 6291456 | tf_op jit(solution)/shard_map/all_to_all | solution.py:74
  111.4 3.6 fusion.76
  115.0 3.3 fusion.32
  118.3 3.1 fusion.35
  121.4 28.3 %all-to-all-done.1 = bf16[16,3,32,1024]{3,2,1,0:T(8,128)(2,1)S(1)} async-done(((bf16[16,3,32,1024]{3,2,1,0:T(8,128)(2,1)}), bf16[16,3,32,1024]{3,2,1,0:T(8,128)(2,1)S(1)}, u32[]{:S(2)}, u32[]{:S(2)}) %all-to-all-start.1) | async-done | bytes 3145760 | tf_op jit(solution)/shard_map/all_to_all | solution.py:74
  149.7 2.7 slice_convert_fusion.2
  152.6 1.0 copy-done.28
  154.0 1.7 convolution_convert_fusion.5
  155.9 2.4 fusion.23
  158.4 2.4 fusion.26
  161.7 1.7 convolution_convert_fusion.4
  163.8 2.4 fusion.14
  166.2 2.4 fusion.17
  169.7 1.7 convolution_convert_fusion.3
  171.5 1.9 multiply_convert_fusion.2
  173.4 2.4 multiply_convert_fusion.10
  176.8 2.7 convolution_convert_fusion.2
  179.6 2.3 multiply_convert_fusion.8
  182.9 2.6 convolution_convert_fusion.1
  185.9 2.3 multiply_convert_fusion.6
  189.2 2.7 convolution_convert_fusion
  191.9 1.9 fusion.30
  194.6 1.1 copy-done.4
  197.9 2.0 fusion.12
  199.9 2.0 add_convert_fusion
  201.9 2.0 pad_maximum_fusion
  203.9 8.4 %all-to-all-start.3 = ((bf16[16,3,32,1024]{3,2,1,0:T(8,128)(2,1)}), bf16[16,3,32,1024]{3,2,1,0:T(8,128)(2,1)S(1)}, u32[]{:S(2)}, u32[]{:S(2)}) async-start(bf16[16,3,32,1024]{3,2,1,0:T(8,128)(2,1)} %pad_maximum_fusion), calls=%async_computation.3 | async-start | bytes 6291456 | tf_op jit(solution)/shard_map/all_to_all | solution.py:110
  212.3 4.8 reduce-scatter.13.cloned.1.call-done
  217.0 59.2 %reduce-scatter.15.cloned.1.call-done = bf16[32,1024]{1,0:T(8,128)(2,1)} async-done(((bf16[512,1024]{1,0:T(8,128)(2,1)}), bf16[32,1024]{1,0:T(8,128)(2,1)}) %reduce-scatter.15.cloned.1.call-update) | async-done | bytes 65552 | tf_op jit(solution)/shard_map/reduce_scatter | solution.py:99
  276.3 58.2 %reduce-scatter.17.cloned.1.call-done = bf16[32,1024]{1,0:T(8,128)(2,1)} async-done(((bf16[512,1024]{1,0:T(8,128)(2,1)}), bf16[32,1024]{1,0:T(8,128)(2,1)}) %reduce-scatter.17.cloned.1.call-update) | async-done | bytes 65552 | tf_op jit(solution)/shard_map/reduce_scatter | solution.py:99
  334.4 1.6 pad_maximum_fusion.3
  336.0 5.1 gather_fusion.3
  341.2 6.0 %gather.18 = bf16[128,10,1024]{2,1,0:T(8,128)(2,1)} reshape(bf16[1280,1024]{1,0:T(8,128)(2,1)} %gather_fusion.3) | data formatting | bytes 5242880 | tf_op jit(solution)/shard_map/gather | solution.py:113
  347.1 5.0 reduce_sum.25
  352.1 42.7 %reduce-scatter.7.cloned.1.call-done = bf16[64,1024]{1,0:T(8,128)(2,1)} async-done(((bf16[1024,1024]{1,0:T(8,128)(2,1)}), bf16[64,1024]{1,0:T(8,128)(2,1)}) %reduce-scatter.7.cloned.1.call-update) | async-done | bytes 131088 | tf_op jit(solution)/shard_map/reduce_scatter | solution.py:90
  394.8 0.9 slice_bitcast_fusion.2
  395.7 59.3 %reduce-scatter.9.cloned.1.call-done = bf16[64,1024]{1,0:T(8,128)(2,1)} async-done(((bf16[1024,1024]{1,0:T(8,128)(2,1)}), bf16[64,1024]{1,0:T(8,128)(2,1)}) %reduce-scatter.9.cloned.1.call-update) | async-done | bytes 131088 | tf_op jit(solution)/shard_map/reduce_scatter | solution.py:90
  455.9 59.3 %reduce-scatter.11.cloned.1.call-done = bf16[64,1024]{1,0:T(8,128)(2,1)} async-done(((bf16[1024,1024]{1,0:T(8,128)(2,1)}), bf16[64,1024]{1,0:T(8,128)(2,1)}) %reduce-scatter.11.cloned.1.call-update) | async-done | bytes 131088 | tf_op jit(solution)/shard_map/reduce_scatter | solution.py:90
  (135 shorter events, 15.8 us)
Async XLA Ops:
  7.2 15.8 %copy-start.27 = (s32[2]{0:T(128)S(1)}, s32[2]{0:T(128)}, u32[]{:S(2)}) copy-start(s32[2]{0:T(128)} %constant.53) | copy-start | bytes 28
  7.2 15.8 %copy-start.26 = (s32[2]{0:T(128)S(1)}, s32[2]{0:T(128)}, u32[]{:S(2)}) copy-start(s32[2]{0:T(128)} %constant.56) | copy-start | bytes 28
  7.2 21.5 %copy-start.25 = (bf16[128,10]{0,1:T(8,128)(2,1)S(1)}, bf16[128,10]{0,1:T(8,128)(2,1)}, u32[]{:S(2)}) copy-start(bf16[128,10]{0,1:T(8,128)(2,1)} %param.10) | copy-start | bytes 7684
  29.0 17.8 %copy-start.24 = (bf16[128,1024]{1,0:T(8,128)(2,1)S(1)}, bf16[128,1024]{1,0:T(8,128)(2,1)}, u32[]{:S(2)}) copy-start(bf16[128,1024]{1,0:T(8,128)(2,1)} %param.7) | copy-start | bytes 786436
  39.2 13.7 %all-to-all-start = ((bf16[16,3,32]{2,1,0:T(4,128)(2,1)}), bf16[16,3,32]{2,1,0:T(4,128)(2,1)S(1)}, u32[]{:S(2)}, u32[]{:S(2)}) async-start(bf16[16,3,32]{2,1,0:T(4,128)(2,1)} %reshape.178), calls=%async_computation | async-start | bytes 32768 | tf_op jit(solution)/shard_map/all_to_all | solution.py:75
  52.9 47.7 %all-to-all-start.2 = ((bf16[16,3,32,1024]{3,2,1,0:T(8,128)(2,1)}), bf16[16,3,32,1024]{3,2,1,0:T(8,128)(2,1)S(1)}, u32[]{:S(2)}, u32[]{:S(2)}) async-start(bf16[16,3,32,1024]{3,2,1,0:T(8,128)(2,1)} %bitcast.7), calls=%async_computation.2 | async-start | bytes 6291456 | tf_op jit(solution)/shard_map/all_to_all | solution.py:73
  100.6 1.7 copy-start
  102.2 47.5 %all-to-all-start.1 = ((bf16[16,3,32,1024]{3,2,1,0:T(8,128)(2,1)}), bf16[16,3,32,1024]{3,2,1,0:T(8,128)(2,1)S(1)}, u32[]{:S(2)}, u32[]{:S(2)}) async-start(bf16[16,3,32,1024]{3,2,1,0:T(8,128)(2,1)} %bitcast.150), calls=%async_computation.1 | async-start | bytes 6291456 | tf_op jit(solution)/shard_map/all_to_all | solution.py:74
  111.2 105.9 %reduce-scatter.13.cloned.1.call-start = ((), (), s32[]{:S(2)}) async-start(), calls=%async_computation.13 | async-start | bytes 1114112 | tf_op jit(solution)/shard_map/reduce_scatter | solution.py:99
  115.0 3.3 copy-start.9
  152.5 1.2 copy-start.28
  152.5 1.5 copy-start.30
  155.8 120.5 %reduce-scatter.15.cloned.1.call-start = ((), (), s32[]{:S(2)}) async-start(), calls=%async_computation.14 | async-start | bytes 1114112 | tf_op jit(solution)/shard_map/reduce_scatter | solution.py:99
  155.9 2.5 copy-start.7
  155.9 4.9 copy-start.2
  158.4 2.6 copy-start.32
  160.7 1.0 copy-start.34
  163.5 171.0 %reduce-scatter.17.cloned.1.call-start = ((), (), s32[]{:S(2)}) async-start(), calls=%async_computation.15 | async-start | bytes 1114112 | tf_op jit(solution)/shard_map/reduce_scatter | solution.py:99
  163.8 2.5 copy-start.5
  163.8 4.9 copy-start.1
  166.2 2.6 copy-start.36
  168.6 1.1 copy-start.38
  171.4 223.4 %reduce-scatter.7.cloned.1.call-start = ((), (), s32[]{:S(2)}) async-start(), calls=%async_computation.10 | async-start | bytes 2228224 | tf_op jit(solution)/shard_map/reduce_scatter | solution.py:90
  171.5 1.9 copy-start.29
  171.5 1.9 copy-start.31
  173.4 3.3 copy-start.10
  175.8 1.0 copy-start.15
  176.8 2.8 copy-start.12
  176.8 2.8 copy-start.33
  176.8 2.8 copy-start.35
  179.5 275.5 %reduce-scatter.9.cloned.1.call-start = ((), (), s32[]{:S(2)}) async-start(), calls=%async_computation.11 | async-start | bytes 2228224 | tf_op jit(solution)/shard_map/reduce_scatter | solution.py:90
  179.6 3.3 copy-start.8
  181.9 1.0 copy-start.18
  182.9 2.9 copy-start.11
  182.9 2.9 copy-start.37
  182.9 2.9 copy-start.39
  185.6 329.6 %reduce-scatter.11.cloned.1.call-start = ((), (), s32[]{:S(2)}) async-start(), calls=%async_computation.12 | async-start | bytes 2228224 | tf_op jit(solution)/shard_map/reduce_scatter | solution.py:90
  185.9 3.3 copy-start.6
  188.2 0.8 copy-start.20
  188.2 1.0 copy-start.22
  189.2 2.7 copy-start.3
  191.9 1.9 copy-start.19
  193.8 1.9 copy-start.4
  193.8 2.0 copy-start.14
  195.8 1.0 copy-start.17
  196.9 1.0 copy-start.23
  197.6 2.3 copy-start.21
  203.9 132.2 %all-to-all-start.3 = ((bf16[16,3,32,1024]{3,2,1,0:T(8,128)(2,1)}), bf16[16,3,32,1024]{3,2,1,0:T(8,128)(2,1)S(1)}, u32[]{:S(2)}, u32[]{:S(2)}) async-start(bf16[16,3,32,1024]{3,2,1,0:T(8,128)(2,1)} %pad_maximum_fusion), calls=%async_computation.3 | async-start | bytes 6291456 | tf_op jit(solution)/shard_map/all_to_all | solution.py:110
  (2 other events, 1.6 us)
Sparse Core Ops, SparseCore 0:
  155.9 61.1 reduce-scatter.12
  219.7 56.5 reduce-scatter.14
  278.8 55.6 reduce-scatter.16
  337.0 57.7 reduce-scatter.6
  397.4 57.5 reduce-scatter.8
  457.5 57.5 reduce-scatter.10
where the time goes:
time: 525 us; the launch traced here: 524 us
  waiting for transfers between devices  346 us (66%)
  local copies, waits for them, and re-layouts  57.4 us (11%)
  matrix products  44.4 us (8%)
  starting transfers between devices  32.5 us (6%)
  other arithmetic  28.8 us (5%)
  between operations  14.7 us (3%)
    reduce_scatter x3, waiting for transfers between devices, shards(): lax.psum_scatter(contract_first(rows_x, d_both).astype(jnp.bfloat16), 'dp...  161 us
    reduce_scatter x3, waiting for transfers between devices, shards(): lax.psum_scatter(contract_first(hidden, d_out).astype(jnp.bfloat16), 'dp'...  122 us
    all_to_all x1, waiting for transfers between devices, shards(): lax.all_to_all(send_x, 'expert', split_axis=0, concat_axis=0, tiled=True)  33.8 us
    all_to_all x1, waiting for transfers between devices, shards(): lax.all_to_all(send_dy, 'expert', split_axis=0, concat_axis=0, tiled=True)  28.3 us
    unnamed x84, local copies, waits for them, and re-layouts  15.7 us
    dot_general x9, matrix products, contract_last(): lax.dot_general(left, right, (((1,), (1,)), ((), ())), preferred_element_...  15.2 us
    another operation x2, other arithmetic  13.6 us
    dot_general x6, matrix products, contract_first(): lax.dot_general(left, right, (((0,), (0,)), ((), ())), preferred_element_...  13.2 us
  transfers between devices with their start and end apart: 10, of which 9 were waited for; matrix products, arithmetic and copies ran while one was open for 16% of the time, Pallas kernels for 0%

commit v1 on v0

v1 whole, which is shorter than its diff:
```python
import functools

import jax
import jax.numpy as jnp
from jax import lax
from jax.experimental import pallas as pl
from jax.experimental.pallas import tpu as pltpu
from jax.sharding import PartitionSpec as P

MESH = pl.DeviceIdType.MESH
BF = jnp.bfloat16
F32 = jnp.float32
SIDE = 4
BATCHES = (
    ((0, 0), (1, 0), (3, 0), (0, 1)),
    ((0, 3), (1, 1), (1, 3), (3, 1)),
    ((3, 3), (2, 0), (0, 2), (2, 1)),
    ((2, 3), (1, 2), (3, 2), (2, 2)),
)


def dot_nn(a, b):
    return lax.dot_general(a, b, (((1,), (0,)), ((), ())), preferred_element_type=F32)


def dot_nt(a, b):
    return lax.dot_general(a, b, (((1,), (1,)), ((), ())), preferred_element_type=F32)


def dot_tn(a, b):
    return lax.dot_general(a, b, (((0,), (0,)), ((), ())), preferred_element_type=F32)


def kernel(
    dims,
    tok_ref, gout_ref, routes_ref, comb_ref, wg_ref, wu_ref, wd_ref,
    gt_out, gg_out, gu_out, gd_out,
    gx, gy, gc, wg, wu, wd, xr, do, hid, dgu, drows, pm,
    t0, t1, ra0, ra1, rb0, rb1, sa0, sa1, sb0, sb1,
    wp, sib, rz,
    local_sem, send_sem, recv_sem,
):
    tok, width, ff, held, cap, top, nz = dims
    half = tok // 2
    hw = width // 2
    rows_b = 4 * cap
    dp = lax.axis_index("dp")
    ex = lax.axis_index("expert")
    core, z = lax.rem(dp, 2), lax.div(dp, 2)
    px, py = lax.rem(ex, SIDE), lax.div(ex, SIDE)

    def near(axis, step):
        if axis == "x":
            return (dp, py * SIDE + lax.rem(px + step + SIDE, SIDE))
        if axis == "y":
            return (dp, lax.rem(py + step + SIDE, SIDE) * SIDE + px)
        if axis == "z":
            return (lax.rem(z + step + nz, nz) * 2 + core, ex)
        return (z * 2 + 1 - core, ex)

    partners = [near("x", 1), near("x", -1), near("y", 1), near("y", -1),
                near("z", 1), near("z", -1), near("core", 1)]

    count = [0]
    sent = []

    def push(src, dst, where):
        k = count[0]
        count[0] += 1
        copy = pltpu.make_async_remote_copy(
            src_ref=src, dst_ref=dst, send_sem=send_sem.at[k], recv_sem=recv_sem.at[k],
            device_id=where, device_id_type=MESH,
        )
        copy.start()
        sent.append(copy)
        return copy

    own_x = pltpu.make_async_copy(tok_ref, gx.at[0], local_sem.at[0])
    own_y = pltpu.make_async_copy(gout_ref, gy.at[0], local_sem.at[1])
    own_x.start()
    own_y.start()
    loads = [pltpu.make_async_copy(a, b, local_sem.at[2 + i])
             for i, (a, b) in enumerate(((wg_ref, wg), (wu_ref, wu), (wd_ref, wd)))]

    barrier = pltpu.get_barrier_semaphore()
    for who in partners:
        pl.semaphore_signal(barrier, inc=1, device_id=who, device_id_type=MESH)

    peers = SIDE * SIDE
    ids = lax.broadcasted_iota(jnp.int32, (peers, tok), 0) * held
    for j in range(held):
        total = jnp.zeros((peers, tok), F32)
        for k in range(top):
            total = total + jnp.where(
                routes_ref[k:k + 1, :] == ids + j, comb_ref[k:k + 1, :].astype(F32), 0.0)
        gc[0, :, j * tok:(j + 1) * tok] = total.astype(BF)

    own_x.wait()
    own_y.wait()
    pl.semaphore_wait(barrier, len(partners))

    arrays = {"c": (gc, "x", "y"), "x": (gx, "x", "y"), "y": (gy, "y", "x")}
    coming = {}

    def slot(name, o1, o2):
        return o2 * SIDE + o1 if arrays[name][1] == "x" else o1 * SIDE + o2

    def hop(name, o1, o2, which, step, part=None):
        ref, axis = arrays[name][0], arrays[name][which]
        if which == 1:
            l1, l2 = (o1 - step) % SIDE, o2
        else:
            l1, l2 = o1, (o2 - step) % SIDE
        src, dst = ref.at[slot(name, o1, o2)], ref.at[slot(name, l1, l2)]
        if part is not None:
            src, dst = src.at[pl.ds(part * half, half)], dst.at[pl.ds(part * half, half)]
        coming.setdefault((name, l1, l2), []).append(push(src, dst, near(axis, step)))

    def onward(name, o1, o2, which, off):
        if name == "c":
            if off == 3:
                hop(name, o1, o2, which, 1)
        else:
            hop(name, o1, o2, which, 1 if off == 3 else -1, 0 if off == 3 else 1)

    def arrive(name, o1, o2):
        for copy in coming[(name, o1, o2)]:
            copy.wait_recv()
        if o2 == 0:
            if o1 in (1, 3):
                onward(name, o1, o2, 1, o1)
            for step in (1, -1):
                hop(name, o1, o2, 2, step)
        elif o2 in (1, 3):
            onward(name, o1, o2, 2, o2)

    for which in (1, 2):
        for name in ("c", "x", "y"):
            for step in (1, -1):
                hop(name, 0, 0, which, step)
    for load in loads:
        load.start()

    def arrivals(*offsets):
        for o1, o2 in offsets:
            for name in ("c", "x", "y"):
                arrive(name, o1, o2)

    lower = lax.broadcasted_iota(jnp.int32, (tok, tok), 0)
    upper = lax.broadcasted_iota(jnp.int32, (tok, tok), 1)
    before = (lower < upper).astype(BF)
    slots_in = lax.broadcasted_iota(jnp.int32, (cap, tok), 0).astype(F32)
    mine = lax.broadcasted_iota(jnp.int32, (peers, held * tok), 0) == ex

    def select(i, ox, oy):
        s = oy * SIDE + ox
        weight = jnp.sum(jnp.where(mine, gc[s].astype(F32), 0.0), axis=0, keepdims=True)
        named = jnp.where(weight > 0.0, 1.0, 0.0)
        picks = []
        for j in range(held):
            lane = named[:, j * tok:(j + 1) * tok]
            rank = dot_nn(jnp.broadcast_to(lane, (16, tok)).astype(BF), before)[0:1, :]
            picks.append(jnp.where((slots_in == rank) & (lane > 0.0), 1.0, 0.0))
        pick = jnp.concatenate(picks, axis=0)
        scaled = jnp.concatenate(
            [picks[j] * weight[:, j * tok:(j + 1) * tok] for j in range(held)], axis=0).astype(BF)
        pick = pick.astype(BF)
        pm[i % 4] = pick
        rows_x = dot_nn(pick, gx[s]).astype(BF)
        rows_d = dot_nn(scaled, gy[s]).astype(BF)
        for j in range(held):
            xr[j, i * cap:(i + 1) * cap, :] = rows_x[j * cap:(j + 1) * cap]
            do[j, i * cap:(i + 1) * cap, :] = rows_d[j * cap:(j + 1) * cap]

    def batch(b):
        sources = BATCHES[b]
        for i, (ox, oy) in enumerate(sources):
            select(4 * b + i, ox, oy)
        rows = slice(b * rows_b, (b + 1) * rows_b)

        def expert(e, carry):
            x, d = xr[e, rows, :], do[e, rows, :]
            gate = dot_nn(x, wg[e])
            up = dot_nn(x, wu[e])
            sg = jax.nn.sigmoid(gate)
            hid[e, rows, :] = (gate * sg * up).astype(BF)
            dh = dot_nt(d, wd[e])
            dgate = (dh * up * sg * (1.0 + gate * (1.0 - sg))).astype(BF)
            dup = (dh * gate * sg).astype(BF)
            dgu[e, rows, 0:ff] = dgate
            dgu[e, rows, ff:2 * ff] = dup
            back = (dot_nt(dgate, wg[e]) + dot_nt(dup, wu[e])).astype(BF)
            for i in range(4):
                drows[i, e] = back[i * cap:(i + 1) * cap]
            return carry

        lax.fori_loop(0, held, expert, 0)
        for i, (ox, oy) in enumerate(sources):
            part = dot_tn(pm[i], drows[i].reshape(held * cap, width)).astype(BF)
            t0[ox, oy] = part[:, 0:hw]
            t1[oy, ox] = part[:, hw:width]

    arrivals((1, 0), (3, 0))
    arrivals((0, 1), (0, 3))
    arrivals((2, 0))
    for load in loads:
        load.wait()
    batch(0)
    arrivals((1, 1), (1, 3), (3, 1), (3, 3))
    batch(1)
    arrivals((0, 2), (2, 1), (2, 3))
    arrivals((1, 2))
    batch(2)
    arrivals((3, 2), (2, 2))
    batch(3)

    def far_send(t, ra, axis):
        return [push(t.at[2, :, pl.ds(0, half)], ra.at[0], near(axis, 1)),
                push(t.at[2, :, pl.ds(half, half)], ra.at[1], near(axis, -1))]

    def near_send(t, ra, rb, axis, copies):
        copies[0].wait_recv()
        copies[1].wait_recv()
        for i in range(SIDE):
            t[1, i, 0:half] = (t[1, i, 0:half].astype(F32) + ra[0, i].astype(F32)).astype(BF)
            t[3, i, half:tok] = (t[3, i, half:tok].astype(F32) + ra[1, i].astype(F32)).astype(BF)
        return [push(t.at[1], rb.at[0], near(axis, 1)), push(t.at[3], rb.at[1], near(axis, -1))]

    def near_sum(t, rb, copies):
        copies[0].wait_recv()
        copies[1].wait_recv()
        for i in range(SIDE):
            t[0, i] = (t[0, i].astype(F32) + rb[0, i].astype(F32) + rb[1, i].astype(F32)).astype(BF)

    def far_send2(t, sa, axis):
        return [push(t.at[0, 2, pl.ds(0, half)], sa.at[0], near(axis, 1)),
                push(t.at[0, 2, pl.ds(half, half)], sa.at[1], near(axis, -1))]

    def near_send2(t, sa, sb, axis, copies):
        copies[0].wait_recv()
        copies[1].wait_recv()
        t[0, 1, 0:half] = (t[0, 1, 0:half].astype(F32) + sa[0].astype(F32)).astype(BF)
        t[0, 3, half:tok] = (t[0, 3, half:tok].astype(F32) + sa[1].astype(F32)).astype(BF)
        return [push(t.at[0, 1], sb.at[0], near(axis, 1)), push(t.at[0, 3], sb.at[1], near(axis, -1))]

    def last_sum(t, sb, at, copies):
        copies[0].wait_recv()
        copies[1].wait_recv()
        gt_out[:, at:at + hw] = (
            t[0, 0].astype(F32) + sb[0].astype(F32) + sb[1].astype(F32)).astype(BF)

    gr, dr = width // (2 * nz), ff // (2 * nz)

    def weights(e):
        def piece(p, carry):
            at = pl.multiple_of(p * 4 * gr, 4 * gr)
            res = dot_tn(xr[e, :, pl.ds(at, 4 * gr)], dgu[e]).astype(BF)
            for zz in range(2):
                for c in range(2):
                    for d in range(2):
                        wp[e, c, d, 2 * p + zz, 0:gr, :] = res[
                            (2 * zz + c) * gr:(2 * zz + c + 1) * gr, d * ff:(d + 1) * ff]
            at = pl.multiple_of(p * 4 * dr, 4 * dr)
            res = dot_tn(hid[e, :, pl.ds(at, 4 * dr)], do[e]).astype(BF)
            for zz in range(2):
                for c in range(2):
                    for d in range(2):
                        wp[e, c, d, 2 * p + zz, gr:gr + dr, :] = res[
                            (2 * zz + c) * dr:(2 * zz + c + 1) * dr, d * hw:(d + 1) * hw]
            return carry

        lax.fori_loop(0, nz // 2, piece, 0)
        return push(wp.at[e, 1 - core], sib.at[e], near("core", 1))

    ring = {}

    def ring_step(e, d, k):
        b = lax.rem(z - 1 - k + 2 * nz, nz) if d == 0 else lax.rem(z + 1 + k, nz)
        total = wp[e, core, d, b].astype(F32) + sib[e, d, b].astype(F32)
        if k > 0:
            ring[(e, d)].wait_recv()
            total = total + rz[e, d, k - 1].astype(F32)
        total = total.astype(BF)
        if k < nz - 1:
            wp[e, core, d, b] = total
            ring[(e, d)] = push(
                wp.at[e, core, d, b], rz.at[e, d, k], near("z", 1 if d == 0 else -1))
        else:
            out = gg_out if d == 0 else gu_out
            out[e] = total[0:gr]
            gd_out[e, :, d * hw:(d + 1) * hw] = total[gr:gr + dr]

    ca0, ca1 = far_send(t0, ra0, "x"), far_send(t1, ra1, "y")
    pair = [weights(0)]
    pair.append(weights(1))
    pair[0].wait_recv()
    ring_step(0, 0, 0)
    ring_step(0, 1, 0)
    cb0 = near_send(t0, ra0, rb0, "x", ca0)
    cb1 = near_send(t1, ra1, rb1, "y", ca1)
    pair.append(weights(2))
    for e in (1, 2):
        pair[e].wait_recv()
        ring_step(e, 0, 0)
        ring_step(e, 1, 0)
    for k in range(1, nz):
        for e in range(held):
            for d in range(2):
                ring_step(e, d, k)
        if k == 1:
            near_sum(t0, rb0, cb0)
            ca0 = far_send2(t0, sa0, "y")
            near_sum(t1, rb1, cb1)
            ca1 = far_send2(t1, sa1, "x")
        if k == 2:
            cb0 = near_send2(t0, sa0, sb0, "y", ca0)
            cb1 = near_send2(t1, sa1, sb1, "x", ca1)
        if k == 3:
            last_sum(t0, sb0, 0, cb0)
            last_sum(t1, sb1, hw, cb1)
    for copy in sent:
        copy.wait_send()


COPIES = 15 + 40 + 16 + 3


def shards(tokens, grad_out, routes, combine, w_gate, w_up, w_down):
    tok, width = tokens.shape
    top = routes.shape[1]
    held, unused, ff = w_gate.shape
    peers = lax.axis_size("expert")
    nz = lax.axis_size("dp") // 2
    cap = 8 * ((tok * top * 6 // (5 * peers * held) + 7) // 8)
    dims = (tok, width, ff, held, cap, top, nz)
    rows, hw, half = peers * cap, width // 2, tok // 2
    block = width // (2 * nz) + ff // (2 * nz)
    copies = COPIES + held * 2 * (nz - 1)
    any_spec = pl.BlockSpec(memory_space=pl.ANY)
    vmem_spec = pl.BlockSpec(memory_space=pltpu.VMEM)
    flops = 16 * rows * held * width * ff
    return pl.pallas_call(
        functools.partial(kernel, dims),
        out_shape=(
            jax.ShapeDtypeStruct((tok, width), BF),
            jax.ShapeDtypeStruct((held, width // (2 * nz), ff), BF),
            jax.ShapeDtypeStruct((held, width // (2 * nz), ff), BF),
            jax.ShapeDtypeStruct((held, ff // (2 * nz), width), BF),
        ),
        in_specs=[any_spec, any_spec, vmem_spec, vmem_spec, any_spec, any_spec, any_spec],
        out_specs=(vmem_spec,) * 4,
        scratch_shapes=[
            pltpu.VMEM((peers, tok, width), BF),
            pltpu.VMEM((peers, tok, width), BF),
            pltpu.VMEM((peers, peers, held * tok), BF),
            pltpu.VMEM((held, width, ff), BF),
            pltpu.VMEM((held, width, ff), BF),
            pltpu.VMEM((held, ff, width), BF),
            pltpu.VMEM((held, rows, width), BF),
            pltpu.VMEM((held, rows, width), BF),
            pltpu.VMEM((held, rows, ff), BF),
            pltpu.VMEM((held, rows, 2 * ff), BF),
            pltpu.VMEM((4, held, cap, width), BF),
            pltpu.VMEM((4, held * cap, tok), BF),
            pltpu.VMEM((SIDE, SIDE, tok, hw), BF),
            pltpu.VMEM((SIDE, SIDE, tok, hw), BF),
            pltpu.VMEM((2, SIDE, half, hw), BF),
            pltpu.VMEM((2, SIDE, half, hw), BF),
            pltpu.VMEM((2, SIDE, tok, hw), BF),
            pltpu.VMEM((2, SIDE, tok, hw), BF),
            pltpu.VMEM((2, half, hw), BF),
            pltpu.VMEM((2, half, hw), BF),
            pltpu.VMEM((2, tok, hw), BF),
            pltpu.VMEM((2, tok, hw), BF),
            pltpu.VMEM((held, 2, 2, nz, block, ff), BF),
            pltpu.VMEM((held, 2, nz, block, ff), BF),
            pltpu.VMEM((held, 2, nz - 1, block, ff), BF),
            pltpu.SemaphoreType.DMA((5,)),
            pltpu.SemaphoreType.DMA((copies,)),
            pltpu.SemaphoreType.DMA((copies,)),
        ],
        cost_estimate=pl.CostEstimate(
            flops=flops, bytes_accessed=12 * 1024 * 1024, transcendentals=rows * held * ff),
        compiler_params=pltpu.CompilerParams(
            collective_id=0, has_side_effects=True, vmem_limit_bytes=62 * 1024 * 1024),
    )(tokens, grad_out, routes.T, combine.T, w_gate, w_up, w_down)


def solution(mesh):
    return jax.shard_map(
        shards,
        mesh=mesh,
        in_specs=(
            P(("dp", "expert"), None),
            P(("dp", "expert"), None),
            P(("dp", "expert"), None),
            P(("dp", "expert"), None),
            P("expert", None, None),
            P("expert", None, None),
            P("expert", None, None),
        ),
        out_specs=(
            P(("dp", "expert"), None),
            P("expert", "dp", None),
            P("expert", "dp", None),
            P("expert", "dp", None),
        ),
        check_vma=False,
    )
```

time: 525 us -> 129 us (0.25)
  waiting for transfers between devices: 346 us -> 0 us
  Pallas kernels: 0 us -> 120 us
  local copies, waits for them, and re-layouts: 57.4 us -> 6.52 us
  matrix products: 44.4 us -> 0 us
  starting transfers between devices: 32.5 us -> 0 us
  other arithmetic: 28.8 us -> 0 us
  between operations: 14.7 us -> 0.64 us
    reduce_scatter x6 -> x0, waiting for transfers between devices: 283 us -> none  [the longest x3 161 us: shards(): lax.psum_scatter(contract_first(rows_x, d_both).astype(jnp.bfloat16), 'dp...]
    pallas_call x0 -> x1, Pallas kernels: none -> 120 us  [shards(): pl.pallas_call(functools.partial(kernel, dims), out_shape=(jax.ShapeDtype...]
    all_to_all x4 -> x0, waiting for transfers between devices: 62.3 us -> none  [the longest x1 33.8 us: shards(): lax.all_to_all(send_x, 'expert', split_axis=0, concat_axis=0, tiled=True)]
    dot_general x21 -> x0, matrix products: 44.4 us -> none  [the longest x9 15.2 us: contract_last(): lax.dot_general(left, right, (((1,), (1,)), ((), ())), preferred_element_...]
    gather x5 -> x0, local copies, waits for them, and re-layouts: 32.2 us -> none  [the longest x2 11.1 us: shards(): flat_back[row_of_pair].astype(jnp.float32)]
    all_to_all x4 -> x0, starting transfers between devices: 31.8 us -> none  [the longest x1 8.92 us: shards(): lax.all_to_all(send_dy, 'expert', split_axis=0, concat_axis=0, tiled=True)]
    another operation x5 -> x0, other arithmetic: 18 us -> none
    unnamed x84 -> x4, local copies, waits for them, and re-layouts: 15.7 us -> 6.52 us
  transfers between devices with their start and end apart: 10 -> 0, of which waited for: 9 -> 0; matrix products, arithmetic and copies ran while one was open for 16% -> 0% of each run, Pallas kernels for 0% -> 0%
where the time goes in v1:
time: 129 us; the launch traced here: 127 us
  Pallas kernels  120 us (93%)
  local copies, waits for them, and re-layouts  6.52 us (5%)
    pallas_call x1, Pallas kernels, shards(): pl.pallas_call(functools.partial(kernel, dims), out_shape=(jax.ShapeDtype...  120 us
    unnamed x4, local copies, waits for them, and re-layouts  6.52 us

profile of v1, /device:TPU:2, one launch (start us, length us, event | category | flops | bytes accessed | tf_op | source)
XLA Modules:
  0.0 127.2 jit_solution(8432858131837060716)
XLA Ops:
  0.6 120.0 %shard_map.102 = (bf16[128,1024]{1,0:T(8,128)(2,1)}, bf16[3,64,512]{2,1,0:T(8,128)(2,1)}, bf16[3,64,512]{2,1,0:T(8,128)(2,1)}, bf16[3,32,1024]{2,1,0:T(8,128)(2,1)}) custom-call(bf16[128,1024]{1,0:T(8,128)(2,1)} %tok_ref.1, bf16[128,1024]{1,0:T(8,128)(2,1)} %gout_ref.1, s32[10,128]{1,0:T(8,128)} %bitcast.2, bf16[10,128]{1,0:T(8,128)(2,1)} %bitcast.3, ...), custom_call_target="tpu_custom_call" | custom-call | flops 12884901888 | bytes 12582912 | tf_op jit(solution)/shard_map/pallas_call | solution.py:342
  120.6 1.7 %copy.15 = bf16[128,1024]{1,0:T(8,128)(2,1)} copy(bf16[128,1024]{1,0:T(8,128)(2,1)} %get-tuple-element.8) | data formatting | bytes 524288
  122.3 1.6 %copy.16 = bf16[3,64,512]{2,1,0:T(8,128)(2,1)} copy(bf16[3,64,512]{2,1,0:T(8,128)(2,1)} %get-tuple-element.9) | data formatting | bytes 393216
  123.9 1.6 %copy.17 = bf16[3,64,512]{2,1,0:T(8,128)(2,1)} copy(bf16[3,64,512]{2,1,0:T(8,128)(2,1)} %get-tuple-element.10) | data formatting | bytes 393216
  125.5 1.6 %copy.18 = bf16[3,32,1024]{2,1,0:T(8,128)(2,1)} copy(bf16[3,32,1024]{2,1,0:T(8,128)(2,1)} %get-tuple-element.11) | data formatting | bytes 393216

commit v2 on v1

v2 whole, which is shorter than its diff:
```python
import functools

import jax
import jax.numpy as jnp
from jax import lax
from jax.experimental import pallas as pl
from jax.experimental.pallas import tpu as pltpu
from jax.sharding import PartitionSpec as P

MESH = pl.DeviceIdType.MESH
BF = jnp.bfloat16
F32 = jnp.float32
SIDE = 4
BATCHES = (
    ((0, 0), (3, 0), (1, 0), (0, 3), (0, 1)),
    ((3, 3), (3, 1), (1, 3), (1, 1), (2, 0), (0, 2)),
    ((2, 3), (2, 1), (3, 2), (1, 2), (2, 2)),
)
STARTS = (0, 5, 11, 16)


def dot_nn(a, b):
    return lax.dot_general(a, b, (((1,), (0,)), ((), ())), preferred_element_type=F32)


def dot_nt(a, b):
    return lax.dot_general(a, b, (((1,), (1,)), ((), ())), preferred_element_type=F32)


def dot_tn(a, b):
    return lax.dot_general(a, b, (((0,), (0,)), ((), ())), preferred_element_type=F32)


def kernel(
    dims,
    tok_ref, gout_ref, routes_ref, comb_ref, wg_ref, wu_ref, wd_ref,
    gt_out, gg_out, gu_out, gd_out,
    gx, gy, gc, wg, wu, wd, xr, do, hid, dgu, drows, pm,
    t0, t1, ra0, ra1, rb0, rb1, sa0, sa1, sb0, sb1,
    wp, sib, rz, dn, dsib, drz,
    local_sem, send_sem, recv_sem,
):
    tok, width, ff, held, cap, top, nz = dims
    half = tok // 2
    hw, qw = width // 2, width // 4
    dp = lax.axis_index("dp")
    ex = lax.axis_index("expert")
    core, z = lax.rem(dp, 2), lax.div(dp, 2)
    px, py = lax.rem(ex, SIDE), lax.div(ex, SIDE)

    def near(axis, step):
        if axis == "x":
            return (dp, py * SIDE + lax.rem(px + step + SIDE, SIDE))
        if axis == "y":
            return (dp, lax.rem(py + step + SIDE, SIDE) * SIDE + px)
        if axis == "z":
            return (lax.rem(z + step + nz, nz) * 2 + core, ex)
        return (z * 2 + 1 - core, ex)

    partners = [near("x", 1), near("x", -1), near("y", 1), near("y", -1),
                near("z", 1), near("z", -1), near("core", 1)]

    count = [0]
    sent = []

    def push(src, dst, where):
        k = count[0]
        count[0] += 1
        copy = pltpu.make_async_remote_copy(
            src_ref=src, dst_ref=dst, send_sem=send_sem.at[k], recv_sem=recv_sem.at[k],
            device_id=where, device_id_type=MESH,
        )
        copy.start()
        sent.append(copy)
        return copy

    owns = [pltpu.make_async_copy(a, b, local_sem.at[i])
            for i, (a, b) in enumerate(((tok_ref, gx.at[0]), (gout_ref, gy.at[0])))]
    for own in owns:
        own.start()
    loads = [pltpu.make_async_copy(a, b, local_sem.at[2 + i])
             for i, (a, b) in enumerate(((wg_ref, wg), (wu_ref, wu), (wd_ref, wd)))]

    barrier = pltpu.get_barrier_semaphore()
    for who in partners:
        pl.semaphore_signal(barrier, inc=1, device_id=who, device_id_type=MESH)

    peers = SIDE * SIDE
    ids = lax.broadcasted_iota(jnp.int32, (peers, tok), 0) * held
    for j in range(held):
        total = jnp.zeros((peers, tok), F32)
        for k in range(top):
            total = total + jnp.where(
                routes_ref[k:k + 1, :] == ids + j, comb_ref[k:k + 1, :].astype(F32), 0.0)
        gc[0, :, j * tok:(j + 1) * tok] = total.astype(BF)

    for own in owns:
        own.wait()
    pl.semaphore_wait(barrier, len(partners))

    arrays = {"c": (gc, "x", "y"), "x": (gx, "x", "y"), "y": (gy, "y", "x")}
    coming = {}

    def slot(name, o1, o2):
        return o2 * SIDE + o1 if arrays[name][1] == "x" else o1 * SIDE + o2

    def hop(name, o1, o2, which, step, far=False):
        ref, axis = arrays[name][0], arrays[name][which]
        l1, l2 = ((o1 - step) % SIDE, o2) if which == 1 else (o1, (o2 - step) % SIDE)
        src, dst = ref.at[slot(name, o1, o2)], ref.at[slot(name, l1, l2)]
        if far and name != "c":
            at = 0 if step == 1 else half
            src, dst = src.at[pl.ds(at, half)], dst.at[pl.ds(at, half)]
        coming.setdefault((name, l1, l2), []).append(push(src, dst, near(axis, step)))

    def begin(name):
        for which in (1, 2):
            for step in (1, -1):
                hop(name, 0, 0, which, step)

    def arrive(name, *offsets):
        for o1, o2 in offsets:
            for copy in coming[(name, o1, o2)]:
                copy.wait_recv()
            which, off = (1, o1) if o2 == 0 else (2, o2)
            if off == 3:
                hop(name, o1, o2, which, 1, True)
            if off == 1 and name != "c":
                hop(name, o1, o2, which, -1, True)
            if which == 1:
                for step in (1, -1):
                    hop(name, o1, o2, 2, step)

    n1, n2, f1 = ((3, 0), (1, 0)), ((0, 3), (0, 1)), ((2, 0),)
    mid, f2, g1, g2, last = ((3, 3), (3, 1), (1, 3), (1, 1)), ((0, 2),), ((2, 3), (2, 1)), ((3, 2), (1, 2)), ((2, 2),)

    begin("c")
    begin("x")
    begin("y")
    for load in loads:
        load.start()

    lower = lax.broadcasted_iota(jnp.int32, (tok, tok), 0)
    upper = lax.broadcasted_iota(jnp.int32, (tok, tok), 1)
    before = (lower < upper).astype(BF)
    slots_in = lax.broadcasted_iota(jnp.int32, (cap, tok), 0).astype(F32)
    mine = lax.broadcasted_iota(jnp.int32, (peers, held * tok), 0) == ex

    def select(b, *which):
        for n in which:
            ox, oy = BATCHES[b][n]
            i, s = STARTS[b] + n, oy * SIDE + ox
            weight = jnp.sum(jnp.where(mine, gc[s].astype(F32), 0.0), axis=0, keepdims=True)
            named = jnp.where(weight > 0.0, 1.0, 0.0)
            taken = []
            for j in range(held):
                lane = named[:, j * tok:(j + 1) * tok]
                rank = dot_nn(jnp.broadcast_to(lane, (16, tok)).astype(BF), before)[0:1, :]
                taken.append(jnp.where((slots_in == rank) & (lane > 0.0), 1.0, 0.0))
            pick = jnp.concatenate(taken, axis=0).astype(BF)
            pm[i] = pick
            scaled = jnp.concatenate(
                [taken[j] * weight[:, j * tok:(j + 1) * tok] for j in range(held)], axis=0).astype(BF)
            rows_x = dot_nn(pick, gx[s]).astype(BF)
            rows_d = dot_nn(scaled, gy[s]).astype(BF)
            for j in range(held):
                xr[j, i * cap:(i + 1) * cap, :] = rows_x[j * cap:(j + 1) * cap]
                do[j, i * cap:(i + 1) * cap, :] = rows_d[j * cap:(j + 1) * cap]

    def hidden_part(b):
        rows = slice(STARTS[b] * cap, STARTS[b + 1] * cap)

        def expert(e, carry):
            x = xr[e, rows, :]
            gate = dot_nn(x, wg[e])
            up = dot_nn(x, wu[e])
            sg = jax.nn.sigmoid(gate)
            hid[e, rows, :] = (gate * sg * up).astype(BF)
            dgu[e, rows, 0:ff] = (up * sg * (1.0 + gate * (1.0 - sg))).astype(BF)
            dgu[e, rows, ff:2 * ff] = (gate * sg).astype(BF)
            return carry

        lax.fori_loop(0, held, expert, 0)

    def gates_part(b):
        rows = slice(STARTS[b] * cap, STARTS[b + 1] * cap)

        def expert(e, carry):
            dh = dot_nt(do[e, rows, :], wd[e])
            dgu[e, rows, 0:ff] = (dh * dgu[e, rows, 0:ff].astype(F32)).astype(BF)
            dgu[e, rows, ff:2 * ff] = (dh * dgu[e, rows, ff:2 * ff].astype(F32)).astype(BF)
            return carry

        lax.fori_loop(0, held, expert, 0)

    def rows_part(b):
        rows = slice(STARTS[b] * cap, STARTS[b + 1] * cap)

        def expert(e, carry):
            back = (dot_nt(dgu[e, rows, 0:ff], wg[e]) + dot_nt(dgu[e, rows, ff:2 * ff], wu[e])).astype(BF)
            for i in range(len(BATCHES[b])):
                drows[i, e] = back[i * cap:(i + 1) * cap]
            return carry

        lax.fori_loop(0, held, expert, 0)
        for i, (ox, oy) in enumerate(BATCHES[b]):
            part = dot_tn(pm[STARTS[b] + i], drows[i].reshape(held * cap, width)).astype(BF)
            t0[ox, oy] = part[:, 0:hw]
            t1[oy, ox] = part[:, hw:width]

    def far_send(t, ra, axis):
        return [push(t.at[2, :, pl.ds(0, half)], ra.at[0], near(axis, 1)),
                push(t.at[2, :, pl.ds(half, half)], ra.at[1], near(axis, -1))]

    def near_send(t, ra, rb, axis, copies):
        copies[0].wait_recv()
        copies[1].wait_recv()
        for i in range(SIDE):
            t[1, i, 0:half] = (t[1, i, 0:half].astype(F32) + ra[0, i].astype(F32)).astype(BF)
            t[3, i, half:tok] = (t[3, i, half:tok].astype(F32) + ra[1, i].astype(F32)).astype(BF)
        return [push(t.at[1], rb.at[0], near(axis, 1)), push(t.at[3], rb.at[1], near(axis, -1))]

    def near_sum(t, rb, copies):
        copies[0].wait_recv()
        copies[1].wait_recv()
        for i in range(SIDE):
            t[0, i] = (t[0, i].astype(F32) + rb[0, i].astype(F32) + rb[1, i].astype(F32)).astype(BF)

    def far_send2(t, sa, axis):
        return [push(t.at[0, 2, pl.ds(0, half)], sa.at[0], near(axis, 1)),
                push(t.at[0, 2, pl.ds(half, half)], sa.at[1], near(axis, -1))]

    def near_send2(t, sa, sb, axis, copies):
        copies[0].wait_recv()
        copies[1].wait_recv()
        t[0, 1, 0:half] = (t[0, 1, 0:half].astype(F32) + sa[0].astype(F32)).astype(BF)
        t[0, 3, half:tok] = (t[0, 3, half:tok].astype(F32) + sa[1].astype(F32)).astype(BF)
        return [push(t.at[0, 1], sb.at[0], near(axis, 1)), push(t.at[0, 3], sb.at[1], near(axis, -1))]

    def last_sum(t, sb, at, copies):
        copies[0].wait_recv()
        copies[1].wait_recv()
        gt_out[:, at:at + hw] = (
            t[0, 0].astype(F32) + sb[0].astype(F32) + sb[1].astype(F32)).astype(BF)

    gr, dr = width // (2 * nz), ff // (2 * nz)

    def gate_up(e):
        def piece(p, carry):
            at = pl.multiple_of(p * 4 * gr, 4 * gr)
            res = dot_tn(xr[e, :, pl.ds(at, 4 * gr)], dgu[e]).astype(BF)
            for q in range(4):
                for d in range(2):
                    wp[q % 2, e, 2 * p + q // 2, d] = res[q * gr:(q + 1) * gr, d * ff:(d + 1) * ff]
            return carry

        lax.fori_loop(0, nz // 2, piece, 0)
        return push(wp.at[1 - core, e], sib.at[e], near("core", 1))

    def down(hi):
        def expert(e, carry):
            res = dot_tn(hid[e], do[e, :, hi * hw:(hi + 1) * hw]).astype(BF)
            for q in range(2 * nz):
                for d in range(2):
                    dn[hi, q % 2, q // 2, d, e] = res[q * dr:(q + 1) * dr, d * qw:(d + 1) * qw]
            return carry

        lax.fori_loop(0, held, expert, 0)
        return push(dn.at[hi, 1 - core], dsib.at[hi], near("core", 1))

    ring = {}

    def ring_block(d, k):
        return lax.rem(z - 1 - k + 2 * nz, nz) if d == 0 else lax.rem(z + 1 + k, nz)

    def ring_step(e, k):
        for d in range(2):
            b = ring_block(d, k)
            total = wp[core, e, b, d].astype(F32) + sib[e, b, d].astype(F32)
            if k > 0:
                ring[(e, d)].wait_recv()
                total = total + rz[e, k - 1, d].astype(F32)
            total = total.astype(BF)
            if k < nz - 1:
                wp[core, e, b, d] = total
                ring[(e, d)] = push(
                    wp.at[core, e, b, d], rz.at[e, k, d], near("z", 1 if d == 0 else -1))
            else:
                out = gg_out if d == 0 else gu_out
                out[e] = total

    def down_step(hi, k):
        for d in range(2):
            b = ring_block(d, k)
            total = dn[hi, core, b, d].astype(F32) + dsib[hi, b, d].astype(F32)
            if k > 0:
                ring[("down", hi, d)].wait_recv()
                total = total + drz[hi, k - 1, d].astype(F32)
            total = total.astype(BF)
            if k < nz - 1:
                dn[hi, core, b, d] = total
                ring[("down", hi, d)] = push(
                    dn.at[hi, core, b, d], drz.at[hi, k, d], near("z", 1 if d == 0 else -1))
            else:
                at = hi * hw + d * qw
                gd_out[:, :, at:at + qw] = total

    def every(*offsets):
        for name in ("c", "x", "y"):
            arrive(name, *offsets)

    low = [None, None]
    pair = [None] * held
    at_ring = [0] * held
    at_down = [0, 0]

    def ring_next(*which):
        for e in which:
            if at_ring[e] == 0:
                pair[e].wait_recv()
            ring_step(e, at_ring[e])
            at_ring[e] += 1

    def down_next(*which):
        for hi in which:
            if at_down[hi] == 0:
                low[hi].wait_recv()
            down_step(hi, at_down[hi])
            at_down[hi] += 1

    every(*n1)
    every(*n2)
    for load in loads:
        load.wait()
    select(0, 0, 1, 2, 3, 4)
    hidden_part(0)
    gates_part(0)
    rows_part(0)
    every(*f1)
    every(*mid)
    every(*f2)
    select(1, 0, 1, 2, 3, 4, 5)
    hidden_part(1)
    gates_part(1)
    every(*g1)
    rows_part(1)
    every(*g2)
    select(2, 0, 1, 2, 3)
    every(*last)
    select(2, 4)
    hidden_part(2)
    low[0] = down(0)
    low[1] = down(1)
    gates_part(2)
    down_next(0, 1)
    pair[0] = gate_up(0)
    down_next(0, 1)
    pair[1] = gate_up(1)
    ring_next(0)
    down_next(0, 1)
    pair[2] = gate_up(2)
    ring_next(1)
    rows_part(2)
    ca0, ca1 = far_send(t0, ra0, "x"), far_send(t1, ra1, "y")
    ring_next(0)
    down_next(0, 1)
    ring_next(2, 1, 0)
    down_next(0, 1)
    ring_next(2)
    cb0 = near_send(t0, ra0, rb0, "x", ca0)
    cb1 = near_send(t1, ra1, rb1, "y", ca1)
    ring_next(1, 0)
    down_next(0, 1)
    ring_next(2, 1, 0)
    down_next(0, 1)
    near_sum(t0, rb0, cb0)
    ca0 = far_send2(t0, sa0, "y")
    near_sum(t1, rb1, cb1)
    ca1 = far_send2(t1, sa1, "x")
    ring_next(2, 1, 0)
    down_next(0, 1)
    cb0 = near_send2(t0, sa0, sb0, "y", ca0)
    cb1 = near_send2(t1, sa1, sb1, "x", ca1)
    ring_next(2, 1, 0)
    last_sum(t0, sb0, 0, cb0)
    last_sum(t1, sb1, hw, cb1)
    ring_next(2, 1, 0)
    ring_next(2, 1, 2)
    for copy in sent:
        copy.wait_send()


def hand_on(*refs):
    copies = [pltpu.make_async_copy(refs[i], refs[4 + i], refs[8].at[i]) for i in range(4)]
    for copy in copies:
        copy.start()
    for copy in copies:
        copy.wait()


COPIES = 15 + 40 + 16


def shards(tokens, grad_out, routes, combine, w_gate, w_up, w_down):
    tok, width = tokens.shape
    top = routes.shape[1]
    held, unused, ff = w_gate.shape
    peers = lax.axis_size("expert")
    nz = lax.axis_size("dp") // 2
    cap = 8 * ((tok * top * 6 // (5 * peers * held) + 7) // 8)
    dims = (tok, width, ff, held, cap, top, nz)
    rows, hw, half = peers * cap, width // 2, tok // 2
    gr, dr = width // (2 * nz), ff // (2 * nz)
    copies = COPIES + (held + 2) * (1 + 2 * (nz - 1))
    any_spec = pl.BlockSpec(memory_space=pl.ANY)
    vmem_spec = pl.BlockSpec(memory_space=pltpu.VMEM)
    flops = 16 * rows * held * width * ff
    found = pl.pallas_call(
        functools.partial(kernel, dims),
        out_shape=(
            jax.ShapeDtypeStruct((tok, width), BF),
            jax.ShapeDtypeStruct((held, width // (2 * nz), ff), BF),
            jax.ShapeDtypeStruct((held, width // (2 * nz), ff), BF),
            jax.ShapeDtypeStruct((held, ff // (2 * nz), width), BF),
        ),
        in_specs=[any_spec, any_spec, vmem_spec, vmem_spec, any_spec, any_spec, any_spec],
        out_specs=(vmem_spec,) * 4,
        scratch_shapes=[
            pltpu.VMEM((peers, tok, width), BF),
            pltpu.VMEM((peers, tok, width), BF),
            pltpu.VMEM((peers, peers, held * tok), BF),
            pltpu.VMEM((held, width, ff), BF),
            pltpu.VMEM((held, width, ff), BF),
            pltpu.VMEM((held, ff, width), BF),
            pltpu.VMEM((held, rows, width), BF),
            pltpu.VMEM((held, rows, width), BF),
            pltpu.VMEM((held, rows, ff), BF),
            pltpu.VMEM((held, rows, 2 * ff), BF),
            pltpu.VMEM((6, held, cap, width), BF),
            pltpu.VMEM((peers, held * cap, tok), BF),
            pltpu.VMEM((SIDE, SIDE, tok, hw), BF),
            pltpu.VMEM((SIDE, SIDE, tok, hw), BF),
            pltpu.VMEM((2, SIDE, half, hw), BF),
            pltpu.VMEM((2, SIDE, half, hw), BF),
            pltpu.VMEM((2, SIDE, tok, hw), BF),
            pltpu.VMEM((2, SIDE, tok, hw), BF),
            pltpu.VMEM((2, half, hw), BF),
            pltpu.VMEM((2, half, hw), BF),
            pltpu.VMEM((2, tok, hw), BF),
            pltpu.VMEM((2, tok, hw), BF),
            pltpu.VMEM((2, held, nz, 2, gr, ff), BF),
            pltpu.VMEM((held, nz, 2, gr, ff), BF),
            pltpu.VMEM((held, nz - 1, 2, gr, ff), BF),
            pltpu.VMEM((2, 2, nz, 2, held, dr, width // 4), BF),
            pltpu.VMEM((2, nz, 2, held, dr, width // 4), BF),
            pltpu.VMEM((2, nz - 1, 2, held, dr, width // 4), BF),
            pltpu.SemaphoreType.DMA((5,)),
            pltpu.SemaphoreType.DMA((copies,)),
            pltpu.SemaphoreType.DMA((copies,)),
        ],
        cost_estimate=pl.CostEstimate(
            flops=flops, bytes_accessed=12 * 1024 * 1024, transcendentals=rows * held * ff),
        compiler_params=pltpu.CompilerParams(
            collective_id=0, has_side_effects=True, vmem_limit_bytes=62 * 1024 * 1024),
    )(tokens, grad_out, routes.T, combine.T, w_gate, w_up, w_down)
    return pl.pallas_call(
        hand_on,
        out_shape=tuple(jax.ShapeDtypeStruct(a.shape, a.dtype) for a in found),
        in_specs=[any_spec] * 4,
        out_specs=(vmem_spec,) * 4,
        scratch_shapes=[pltpu.SemaphoreType.DMA((4,))],
    )(*found)


def solution(mesh):
    return jax.shard_map(
        shards,
        mesh=mesh,
        in_specs=(
            P(("dp", "expert"), None),
            P(("dp", "expert"), None),
            P(("dp", "expert"), None),
            P(("dp", "expert"), None),
            P("expert", None, None),
            P("expert", None, None),
            P("expert", None, None),
        ),
        out_specs=(
            P(("dp", "expert"), None),
            P("expert", "dp", None),
            P("expert", "dp", None),
            P("expert", "dp", None),
        ),
        check_vma=False,
    )
```

time: 129 us -> 120 us (0.930)
  local copies, waits for them, and re-layouts: 6.52 us -> 0 us
  Pallas kernels: 120 us -> 118 us
    unnamed x4 -> x0, local copies, waits for them, and re-layouts: 6.52 us -> none
    pallas_call x1, Pallas kernels: 120 us -> 116 us  [shards(): pl.pallas_call(functools.partial(kernel, dims), out_shape=(jax.ShapeDtype...]
    pallas_call x0 -> x1, Pallas kernels: none -> 2.12 us  [shards(): pl.pallas_call(hand_on, out_shape=tuple((jax.ShapeDtypeStruct(a.shape, a....]
where the time goes in v2:
time: 120 us; the launch traced here: 119 us
  Pallas kernels  118 us (98%)
    pallas_call x1, Pallas kernels, shards(): pl.pallas_call(functools.partial(kernel, dims), out_shape=(jax.ShapeDtype...  116 us

profile of v2, /device:TPU:2, one launch (start us, length us, event | category | flops | bytes accessed | tf_op | source)
XLA Modules:
  0.0 119.0 jit_solution(4271816160414643621)
XLA Ops:
  0.6 116.0 %shard_map.102 = (bf16[128,1024]{1,0:T(8,128)(2,1)}, bf16[3,64,512]{2,1,0:T(8,128)(2,1)}, bf16[3,64,512]{2,1,0:T(8,128)(2,1)}, bf16[3,32,1024]{2,1,0:T(8,128)(2,1)}) custom-call(bf16[128,1024]{1,0:T(8,128)(2,1)} %tok_ref.1, bf16[128,1024]{1,0:T(8,128)(2,1)} %gout_ref.1, s32[10,128]{1,0:T(8,128)} %bitcast.2, bf16[10,128]{1,0:T(8,128)(2,1)} %bitcast.3, ...), custom_call_target="tpu_custom_call" | custom-call | flops 12884901888 | bytes 12582912 | tf_op jit(solution)/shard_map/pallas_call | solution.py:418
  116.7 2.1 %shard_map.103 = (bf16[128,1024]{1,0:T(8,128)(2,1)}, bf16[3,64,512]{2,1,0:T(8,128)(2,1)}, bf16[3,64,512]{2,1,0:T(8,128)(2,1)}, bf16[3,32,1024]{2,1,0:T(8,128)(2,1)}) custom-call(bf16[128,1024]{1,0:T(8,128)(2,1)} %get-tuple-element.8.refs_0_, bf16[3,64,512]{2,1,0:T(8,128)(2,1)} %get-tuple-element.9.refs_1_, bf16[3,64,512]{2,1,0:T(8,128)(2,1)} %get-tuple-element.10.refs_2_, ...), custom_call_target="tpu_custom_call" | custom-call | tf_op jit(solution)/shard_map/pallas_call | solution.py:466

commit v3 on v2

--- a/solution.py
+++ b/solution.py
@@ -42,7 +42,8 @@
 ):
     tok, width, ff, held, cap, top, nz = dims
     half = tok // 2
-    hw, qw = width // 2, width // 4
+    peers = SIDE * SIDE
+    hw = width // 2
     dp = lax.axis_index("dp")
     ex = lax.axis_index("expert")
     core, z = lax.rem(dp, 2), lax.div(dp, 2)
@@ -84,15 +85,6 @@
     barrier = pltpu.get_barrier_semaphore()
     for who in partners:
         pl.semaphore_signal(barrier, inc=1, device_id=who, device_id_type=MESH)
-
-    peers = SIDE * SIDE
-    ids = lax.broadcasted_iota(jnp.int32, (peers, tok), 0) * held
-    for j in range(held):
-        total = jnp.zeros((peers, tok), F32)
-        for k in range(top):
-            total = total + jnp.where(
-                routes_ref[k:k + 1, :] == ids + j, comb_ref[k:k + 1, :].astype(F32), 0.0)
-        gc[0, :, j * tok:(j + 1) * tok] = total.astype(BF)
 
     for own in owns:
         own.wait()
@@ -134,8 +126,17 @@
     n1, n2, f1 = ((3, 0), (1, 0)), ((0, 3), (0, 1)), ((2, 0),)
     mid, f2, g1, g2, last = ((3, 3), (3, 1), (1, 3), (1, 1)), ((0, 2),), ((2, 3), (2, 1)), ((3, 2), (1, 2)), ((2, 2),)
 
+    begin("x")
+
+    ids = lax.broadcasted_iota(jnp.int32, (peers, tok), 0) * held
+    for j in range(held):
+        total = jnp.zeros((peers, tok), F32)
+        for k in range(top):
+            total = total + jnp.where(
+                routes_ref[k:k + 1, :] == ids + j, comb_ref[k:k + 1, :].astype(F32), 0.0)
+        gc[0, :, j * tok:(j + 1) * tok] = total.astype(BF)
+
     begin("c")
-    begin("x")
     begin("y")
     for load in loads:
         load.start()
@@ -167,7 +168,7 @@
                 xr[j, i * cap:(i + 1) * cap, :] = rows_x[j * cap:(j + 1) * cap]
                 do[j, i * cap:(i + 1) * cap, :] = rows_d[j * cap:(j + 1) * cap]
 
-    def hidden_part(b):
+    def hidden_part(b, *experts):
         rows = slice(STARTS[b] * cap, STARTS[b + 1] * cap)
 
         def expert(e, carry):
@@ -180,9 +181,12 @@
             dgu[e, rows, ff:2 * ff] = (gate * sg).astype(BF)
             return carry
 
-        lax.fori_loop(0, held, expert, 0)
-
-    def gates_part(b):
+        if experts:
+            expert(experts[0], 0)
+        else:
+            lax.fori_loop(0, held, expert, 0)
+
+    def gates_part(b, *experts):
         rows = slice(STARTS[b] * cap, STARTS[b + 1] * cap)
 
         def expert(e, carry):
@@ -191,9 +195,12 @@
             dgu[e, rows, ff:2 * ff] = (dh * dgu[e, rows, ff:2 * ff].astype(F32)).astype(BF)
             return carry
 
-        lax.fori_loop(0, held, expert, 0)
-
-    def rows_part(b):
+        if experts:
+            expert(experts[0], 0)
+        else:
+            lax.fori_loop(0, held, expert, 0)
+
+    def rows_part(b, *experts):
         rows = slice(STARTS[b] * cap, STARTS[b + 1] * cap)
 
         def expert(e, carry):
@@ -202,7 +209,15 @@
                 drows[i, e] = back[i * cap:(i + 1) * cap]
             return carry
 
-        lax.fori_loop(0, held, expert, 0)
+        if experts:
+            expert(experts[0], 0)
+        else:
+            lax.fori_loop(0, held, expert, 0)
+        if experts:
+            return
+        token_part(b)
+
+    def token_part(b):
         for i, (ox, oy) in enumerate(BATCHES[b]):
             part = dot_tn(pm[STARTS[b] + i], drows[i].reshape(held * cap, width)).astype(BF)
             t0[ox, oy] = part[:, 0:hw]
@@ -257,16 +272,12 @@
         lax.fori_loop(0, nz // 2, piece, 0)
         return push(wp.at[1 - core, e], sib.at[e], near("core", 1))
 
-    def down(hi):
-        def expert(e, carry):
-            res = dot_tn(hid[e], do[e, :, hi * hw:(hi + 1) * hw]).astype(BF)
-            for q in range(2 * nz):
-                for d in range(2):
-                    dn[hi, q % 2, q // 2, d, e] = res[q * dr:(q + 1) * dr, d * qw:(d + 1) * qw]
-            return carry
-
-        lax.fori_loop(0, held, expert, 0)
-        return push(dn.at[hi, 1 - core], dsib.at[hi], near("core", 1))
+    def down(e):
+        res = dot_tn(hid[e], do[e]).astype(BF)
+        for q in range(2 * nz):
+            for d in range(2):
+                dn[q % 2, e, q // 2, d] = res[q * dr:(q + 1) * dr, d * hw:(d + 1) * hw]
+        return push(dn.at[1 - core, e], dsib.at[e], near("core", 1))
 
     ring = {}
 
@@ -289,30 +300,29 @@
                 out = gg_out if d == 0 else gu_out
                 out[e] = total
 
-    def down_step(hi, k):
+    def down_step(e, k):
         for d in range(2):
             b = ring_block(d, k)
-            total = dn[hi, core, b, d].astype(F32) + dsib[hi, b, d].astype(F32)
+            total = dn[core, e, b, d].astype(F32) + dsib[e, b, d].astype(F32)
             if k > 0:
-                ring[("down", hi, d)].wait_recv()
-                total = total + drz[hi, k - 1, d].astype(F32)
+                ring[("down", e, d)].wait_recv()
+                total = total + drz[e, k - 1, d].astype(F32)
             total = total.astype(BF)
             if k < nz - 1:
-                dn[hi, core, b, d] = total
-                ring[("down", hi, d)] = push(
-                    dn.at[hi, core, b, d], drz.at[hi, k, d], near("z", 1 if d == 0 else -1))
+                dn[core, e, b, d] = total
+                ring[("down", e, d)] = push(
+                    dn.at[core, e, b, d], drz.at[e, k, d], near("z", 1 if d == 0 else -1))
             else:
-                at = hi * hw + d * qw
-                gd_out[:, :, at:at + qw] = total
+                gd_out[e, :, d * hw:(d + 1) * hw] = total
 
     def every(*offsets):
         for name in ("c", "x", "y"):
             arrive(name, *offsets)
 
-    low = [None, None]
+    low = [None] * held
     pair = [None] * held
     at_ring = [0] * held
-    at_down = [0, 0]
+    at_down = [0] * held
 
     def ring_next(*which):
         for e in which:
@@ -322,14 +332,15 @@
             at_ring[e] += 1
 
     def down_next(*which):
-        for hi in which:
-            if at_down[hi] == 0:
-                low[hi].wait_recv()
-            down_step(hi, at_down[hi])
-            at_down[hi] += 1
-
-    every(*n1)
-    every(*n2)
+        for e in which:
+            if at_down[e] == 0:
+                low[e].wait_recv()
+            down_step(e, at_down[e])
+            at_down[e] += 1
+
+    arrive("x", *n1, *n2)
+    arrive("c", *n1, *n2)
+    arrive("y", *n1, *n2)
     for load in loads:
         load.wait()
     select(0, 0, 1, 2, 3, 4)
@@ -348,44 +359,56 @@
     select(2, 0, 1, 2, 3)
     every(*last)
     select(2, 4)
-    hidden_part(2)
+    hidden_part(2, 0)
     low[0] = down(0)
+    hidden_part(2, 1)
     low[1] = down(1)
-    gates_part(2)
-    down_next(0, 1)
+    down_next(0)
+    hidden_part(2, 2)
+    low[2] = down(2)
+    down_next(1, 0)
+    gates_part(2, 0)
     pair[0] = gate_up(0)
-    down_next(0, 1)
+    down_next(2, 1, 0)
+    gates_part(2, 1)
     pair[1] = gate_up(1)
     ring_next(0)
-    down_next(0, 1)
+    down_next(2, 1, 0)
+    gates_part(2, 2)
     pair[2] = gate_up(2)
-    ring_next(1)
-    rows_part(2)
+    ring_next(1, 0)
+    down_next(2, 1, 0)
+    rows_part(2, 0)
+    ring_next(2)
+    rows_part(2, 1)
+    ring_next(1, 0)
+    down_next(2, 1, 0)
+    rows_part(2, 2)
+    token_part(2)
     ca0, ca1 = far_send(t0, ra0, "x"), far_send(t1, ra1, "y")
-    ring_next(0)
-    down_next(0, 1)
     ring_next(2, 1, 0)
-    down_next(0, 1)
-    ring_next(2)
+    down_next(2, 1, 0)
+    ring_next(2, 1, 0)
     cb0 = near_send(t0, ra0, rb0, "x", ca0)
     cb1 = near_send(t1, ra1, rb1, "y", ca1)
-    ring_next(1, 0)
-    down_next(0, 1)
+    down_next(2, 1, 0)
     ring_next(2, 1, 0)
-    down_next(0, 1)
+    down_next(2, 1)
+    ring_next(2, 1)
     near_sum(t0, rb0, cb0)
     ca0 = far_send2(t0, sa0, "y")
     near_sum(t1, rb1, cb1)
     ca1 = far_send2(t1, sa1, "x")
-    ring_next(2, 1, 0)
-    down_next(0, 1)
+    ring_next(0)
+    down_next(2)
+    ring_next(2, 1)
     cb0 = near_send2(t0, sa0, sb0, "y", ca0)
     cb1 = near_send2(t1, sa1, sb1, "x", ca1)
-    ring_next(2, 1, 0)
+    ring_next(0, 2, 1)
     last_sum(t0, sb0, 0, cb0)
     last_sum(t1, sb1, hw, cb1)
-    ring_next(2, 1, 0)
-    ring_next(2, 1, 2)
+    ring_next(2)
+    assert at_ring == [nz] * held and at_down == [nz] * held, (at_ring, at_down)
     for copy in sent:
         copy.wait_send()
 
@@ -411,7 +434,7 @@
     dims = (tok, width, ff, held, cap, top, nz)
     rows, hw, half = peers * cap, width // 2, tok // 2
     gr, dr = width // (2 * nz), ff // (2 * nz)
-    copies = COPIES + (held + 2) * (1 + 2 * (nz - 1))
+    copies = COPIES + 2 * held * (1 + 2 * (nz - 1))
     any_spec = pl.BlockSpec(memory_space=pl.ANY)
     vmem_spec = pl.BlockSpec(memory_space=pltpu.VMEM)
     flops = 16 * rows * held * width * ff
@@ -451,9 +474,9 @@
             pltpu.VMEM((2, held, nz, 2, gr, ff), BF),
             pltpu.VMEM((held, nz, 2, gr, ff), BF),
             pltpu.VMEM((held, nz - 1, 2, gr, ff), BF),
-            pltpu.VMEM((2, 2, nz, 2, held, dr, width // 4), BF),
-            pltpu.VMEM((2, nz, 2, held, dr, width // 4), BF),
-            pltpu.VMEM((2, nz - 1, 2, held, dr, width // 4), BF),
+            pltpu.VMEM((2, held, nz, 2, dr, hw), BF),
+            pltpu.VMEM((held, nz, 2, dr, hw), BF),
+            pltpu.VMEM((held, nz - 1, 2, dr, hw), BF),
             pltpu.SemaphoreType.DMA((5,)),
             pltpu.SemaphoreType.DMA((copies,)),
             pltpu.SemaphoreType.DMA((copies,)),

time: 120 us -> 118 us (0.983)
    pallas_call x1, Pallas kernels: 116 us -> 114 us  [shards(): pl.pallas_call(functools.partial(kernel, dims), out_shape=(jax.ShapeDtype...]
where the time goes in v3:
time: 118 us; the launch traced here: 117 us
  Pallas kernels  117 us (99%)
    pallas_call x1, Pallas kernels, shards(): pl.pallas_call(functools.partial(kernel, dims), out_shape=(jax.ShapeDtype...  114 us

profile of v3, /device:TPU:2, one launch (start us, length us, event | category | flops | bytes accessed | tf_op | source)
XLA Modules:
  0.0 117.4 jit_solution(13375147169358476401)
XLA Ops:
  0.6 114.5 %shard_map.102 = (bf16[128,1024]{1,0:T(8,128)(2,1)}, bf16[3,64,512]{2,1,0:T(8,128)(2,1)}, bf16[3,64,512]{2,1,0:T(8,128)(2,1)}, bf16[3,32,1024]{2,1,0:T(8,128)(2,1)}) custom-call(bf16[128,1024]{1,0:T(8,128)(2,1)} %tok_ref.1, bf16[128,1024]{1,0:T(8,128)(2,1)} %gout_ref.1, s32[10,128]{1,0:T(8,128)} %bitcast.2, bf16[10,128]{1,0:T(8,128)(2,1)} %bitcast.3, ...), custom_call_target="tpu_custom_call" | custom-call | flops 12884901888 | bytes 12582912 | tf_op jit(solution)/shard_map/pallas_call | solution.py:441
  115.1 2.1 %shard_map.103 = (bf16[128,1024]{1,0:T(8,128)(2,1)}, bf16[3,64,512]{2,1,0:T(8,128)(2,1)}, bf16[3,64,512]{2,1,0:T(8,128)(2,1)}, bf16[3,32,1024]{2,1,0:T(8,128)(2,1)}) custom-call(bf16[128,1024]{1,0:T(8,128)(2,1)} %get-tuple-element.8.refs_0_, bf16[3,64,512]{2,1,0:T(8,128)(2,1)} %get-tuple-element.9.refs_1_, bf16[3,64,512]{2,1,0:T(8,128)(2,1)} %get-tuple-element.10.refs_2_, ...), custom_call_target="tpu_custom_call" | custom-call | tf_op jit(solution)/shard_map/pallas_call | solution.py:489

commit v4 on v3

--- a/solution.py
+++ b/solution.py
@@ -86,8 +86,7 @@
     for who in partners:
         pl.semaphore_signal(barrier, inc=1, device_id=who, device_id_type=MESH)
 
-    for own in owns:
-        own.wait()
+    owns[0].wait()
     pl.semaphore_wait(barrier, len(partners))
 
     arrays = {"c": (gc, "x", "y"), "x": (gx, "x", "y"), "y": (gy, "y", "x")}
@@ -137,6 +136,7 @@
         gc[0, :, j * tok:(j + 1) * tok] = total.astype(BF)
 
     begin("c")
+    owns[1].wait()
     begin("y")
     for load in loads:
         load.start()

time: 118 us -> 118 us (level)
  no operation moved by 1% of the time
where the time goes in v4:
time: 118 us; the launch traced here: 117 us
  Pallas kernels  116 us (98%)
    pallas_call x1, Pallas kernels, shards(): pl.pallas_call(functools.partial(kernel, dims), out_shape=(jax.ShapeDtype...  114 us

profile of v4, /device:TPU:2, one launch (start us, length us, event | category | flops | bytes accessed | tf_op | source)
XLA Modules:
  0.0 117.2 jit_solution(8631092659771773639)
XLA Ops:
  0.6 114.2 %shard_map.102 = (bf16[128,1024]{1,0:T(8,128)(2,1)}, bf16[3,64,512]{2,1,0:T(8,128)(2,1)}, bf16[3,64,512]{2,1,0:T(8,128)(2,1)}, bf16[3,32,1024]{2,1,0:T(8,128)(2,1)}) custom-call(bf16[128,1024]{1,0:T(8,128)(2,1)} %tok_ref.1, bf16[128,1024]{1,0:T(8,128)(2,1)} %gout_ref.1, s32[10,128]{1,0:T(8,128)} %bitcast.2, bf16[10,128]{1,0:T(8,128)(2,1)} %bitcast.3, ...), custom_call_target="tpu_custom_call" | custom-call | flops 12884901888 | bytes 12582912 | tf_op jit(solution)/shard_map/pallas_call | solution.py:441
  114.9 2.1 %shard_map.103 = (bf16[128,1024]{1,0:T(8,128)(2,1)}, bf16[3,64,512]{2,1,0:T(8,128)(2,1)}, bf16[3,64,512]{2,1,0:T(8,128)(2,1)}, bf16[3,32,1024]{2,1,0:T(8,128)(2,1)}) custom-call(bf16[128,1024]{1,0:T(8,128)(2,1)} %get-tuple-element.8.refs_0_, bf16[3,64,512]{2,1,0:T(8,128)(2,1)} %get-tuple-element.9.refs_1_, bf16[3,64,512]{2,1,0:T(8,128)(2,1)} %get-tuple-element.10.refs_2_, ...), custom_call_target="tpu_custom_call" | custom-call | tf_op jit(solution)/shard_map/pallas_call | solution.py:489
